TPU v7x, 128 devices: a whole 4x4x4 slice. The times are simulated.
128 devices in a mesh: ctx: 16 (over y, x), ch: 8 (over z, core).
Axes of the slice: x: 4, y: 4, z: 4, core: 2. Of those that a mesh axis runs over, the one named last changes fastest.
Arguments:
- tokens: bfloat16 [8192, 8192], P('ctx', 'ch'), may hold values from -6 to 6
- in_weight: bfloat16 [8192, 3, 4096], P('ch', None, 'ctx'), may hold values from -0.09375 to 0.09375
- short_taps: float32 [7, 3, 4096], P(None, None, 'ch'), may hold values from -2 to 2
- residues: float32 [16, 4096], P(None, 'ch'), may hold values from -1.5 to 1.5
- decay_scale: float32 [16, 4096], P(None, 'ch'), may hold values from 0.2 to 512, as said below
- skip_gain: float32 [4096], P('ch'), may hold values from -4 to 4
Outputs:
- filtered: bfloat16 [8192, 4096], P('ctx', 'ch')
Inputs may be any that keep to these rules, and one draw needn't show every extreme that they name: decay_scale[r, c] / 8192 is the fraction by which mode r of channel c fades per position.
All inputs are finite; a program needn't handle non-finite values.
Results may differ from a plain program's by a relative error of at most 0.035.
Values may be sent and summed in bfloat16 or wider, within the bound.
No kernel may reach another device: no remote copies, remote signals or barrier semaphores. Data moves between devices by JAX's collectives and lax.ppermute only.
A program may use at most 128 MiB of HBM per device.

v0:
```python
import math
import jax
import jax.numpy as jnp
from jax import lax
from jax.sharding import PartitionSpec as P

SHORT = 7


def passed_along(value, axis, steps):
    count = lax.axis_size(axis)
    initial, last = (max(0, -steps), min(count, count - steps))
    return lax.ppermute(value, axis, [(source, source + steps) for source in range(initial, last)])


def on_device(tokens, in_weight, short_taps, residues, decay_scale, skip_gain):
    length = tokens.shape[0]
    partial_value = jnp.einsum(
        "td,dmg->tmg",
        tokens,
        lax.all_gather(in_weight, "ctx", axis=2, tiled=True),
        preferred_element_type=jnp.float32,
    )
    projected = lax.psum_scatter(
        partial_value.astype(jnp.bfloat16), "ch", scatter_dimension=2, tiled=True
    )
    previous = passed_along(projected[length - (SHORT - 1) :], "ctx", 1)
    extended = jnp.concatenate([previous, projected], axis=0).astype(jnp.float32)
    smoothed = short_taps[0] * extended[SHORT - 1 : SHORT - 1 + length]
    for offset in range(1, SHORT):
        smoothed = (
            smoothed
            + short_taps[offset] * extended[SHORT - 1 - offset : SHORT - 1 - offset + length]
        )
    gate_part = smoothed[:, 0, :]
    source = smoothed[:, 1, :] * smoothed[:, 2, :]
    channels = source.shape[1]
    seq_total = length * lax.axis_size("ctx")
    decay_rate = decay_scale / seq_total
    mode_weight = residues * jnp.sqrt(-jnp.expm1(-2.0 * decay_rate))
    offsets = jnp.arange(length, dtype=jnp.float32)
    fading = jnp.exp(-decay_rate[:, None, :] * offsets[None, :, None])
    kernel = jnp.sum(fading * mode_weight[:, None, :], axis=0)
    highest = lax.Precision.HIGHEST
    block_len = math.gcd(length, 64)
    block_count = length // block_len
    pieces = source.reshape(block_count, block_len, channels)
    lag_steps = (
        jnp.arange(block_len, dtype=jnp.int32)[:, None]
        - jnp.arange(block_len, dtype=jnp.int32)[None, :]
    )
    toeplitz = jnp.where((lag_steps >= 0)[:, :, None], kernel[jnp.maximum(lag_steps, 0)], 0.0)
    within = jnp.einsum("tsc,jsc->jtc", toeplitz, pieces, precision=highest)
    block_steps = jnp.arange(block_len, dtype=jnp.float32)
    closing = jnp.exp(-decay_rate[:, None, :] * (block_len - 1.0 - block_steps)[None, :, None])
    block_ends = jnp.einsum("rsc,jsc->jrc", closing, pieces, precision=highest)
    block_ids = jnp.arange(block_count, dtype=jnp.int32)
    block_gap = block_ids[:, None] - 1 - block_ids[None, :]
    gap_float = jnp.maximum(block_gap, 0).astype(jnp.float32)
    passing = jnp.exp(-(decay_rate * block_len)[None, None, :, :] * gap_float[:, :, None, None])
    passing = jnp.where((block_gap >= 0)[:, :, None, None], passing, 0.0)
    block_starts = jnp.einsum("jirc,irc->jrc", passing, block_ends, precision=highest)
    opening = jnp.exp(-decay_rate[:, None, :] * (block_steps + 1.0)[None, :, None])
    within = within + jnp.einsum(
        "rtc,jrc->jtc", opening, mode_weight[None, :, :] * block_starts, precision=highest
    )
    local_conv = within.reshape(length, channels)
    tail_decay = jnp.exp(-decay_rate[:, None, :] * (length - 1.0 - offsets)[None, :, None])
    end_state = jnp.sum(tail_decay * source[None, :, :], axis=1)
    states = lax.all_gather(end_state[None].astype(jnp.bfloat16), "ctx", axis=0, tiled=True).astype(
        jnp.float32
    )
    position = lax.axis_index("ctx")
    earlier_ids = jnp.arange(states.shape[0], dtype=jnp.int32)
    distance = jnp.maximum(position - 1 - earlier_ids, 0).astype(jnp.float32)
    weights = jnp.exp(-(decay_rate * length)[None, :, :] * distance[:, None, None])
    weights = jnp.where((earlier_ids < position)[:, None, None], weights, 0.0)
    incoming = jnp.sum(weights * states, axis=0)
    lead_decay = jnp.exp(-decay_rate[:, None, :] * (offsets + 1.0)[None, :, None])
    carried = jnp.sum(lead_decay * (mode_weight * incoming)[:, None, :], axis=0)
    convolved = local_conv + carried
    return (gate_part * (convolved + skip_gain[None, :] * source)).astype(jnp.bfloat16)


def solution(mesh):
    return jax.shard_map(
        on_device,
        mesh=mesh,
        in_specs=(
            P("ctx", "ch"),
            P("ch", None, "ctx"),
            P(None, None, "ch"),
            P(None, "ch"),
            P(None, "ch"),
            P("ch"),
        ),
        out_specs=P("ctx", "ch"),
        check_vma=False,
    )
```

profile of v0, /device:TPU:0, one launch (start us, length us, event | category | flops | bytes accessed | tf_op | source)
XLA Modules:
  0.0 418.5 jit_solution(9464340326151091559)
XLA Ops:
  6.5 0.0 copy-start
  6.5 0.0 all-gather.3.cloned.1.call-start
  6.5 0.7 all-gather.3.cloned.1.call-update
  7.3 0.0 reduce-scatter.2.cloned.1.call-start
  7.3 168.3 %all-gather.3.cloned.1.call-done = bf16[1024,3,4096]{2,0,1:T(8,128)(2,1)} async-done(((bf16[1024,3,256]{2,0,1:T(8,128)(2,1)}), bf16[1024,3,4096]{2,0,1:T(8,128)(2,1)}) %all-gather.3.cloned.1.call-update) | async-done | bytes 25165840 | tf_op jit(solution)/shard_map/all_gather | solution.py:21
  175.6 0.0 copy-done
  175.6 23.7 %convolution_convert_fusion = bf16[512,3,4096]{2,0,1:T(8,128)(2,1)} fusion(bf16[1024,3,4096]{2,0,1:T(8,128)(2,1)} %all-gather.3.cloned.1.call-done, bf16[512,1024]{1,0:T(8,128)(2,1)S(1)} %copy-done), kind=kOutput, calls=%fused_computation.6 | convolution fusion | flops 12891193344 | bytes 38797312 | tf_op jit(solution)/shard_map/td,dmg->tmg/dot_general | solution.py:18
  199.3 0.0 copy-start.6
  199.3 0.0 copy-start.5
  199.3 0.0 reduce-scatter.2.cloned.1.call-update
  199.3 0.1 reshape.140
  199.5 0.6 fusion.35
  200.1 0.1 maximum_convert_fusion.1
  200.2 0.0 copy-done.6
  200.3 0.0 copy-done.5
  200.3 71.2 %reduce-scatter.2.cloned.1.call-done = bf16[512,3,512]{2,0,1:T(8,128)(2,1)} async-done(((bf16[512,3,4096]{2,0,1:T(8,128)(2,1)}), bf16[512,3,512]{2,0,1:T(8,128)(2,1)}) %reduce-scatter.2.cloned.1.call-update) | async-done | bytes 1572880 | tf_op jit(solution)/shard_map/reduce_scatter | solution.py:24
  271.5 0.7 slice.74
  272.3 3.4 collective-permute-start
  275.7 0.1 copy.20
  275.8 1.3 collective-permute-done
  277.2 1.9 maximum_convert_fusion
  279.1 2.6 fusion.10
  281.7 0.0 copy-start.2
  281.7 0.2 fusion.42
  281.9 0.2 slice_multiply_fusion.7
  282.1 1.3 copy-done.2
  283.4 2.9 multiply_reduce_fusion.1
  286.3 28.4 %all-gather = bf16[256,512]{1,0:T(8,128)(2,1)} all-gather(bf16[16,512]{1,0:T(8,128)(2,1)S(1)} %multiply_reduce_fusion.1), channel_id=2, replica_groups=mesh['ctx'=16,'ch'=8] {'ctx'}, dimensions={0}, use_global_device_ids=true | all-gather | bytes 278528 | tf_op jit(solution)/shard_map/all_gather | solution.py:70
  314.7 0.8 copy.18
  315.5 1.1 fusion.34
  316.6 1.4 fusion.37
  318.0 0.8 copy.19
  318.9 7.8 %multiply_reduce_fusion.2 = (f32[512,512]{1,0:T(8,128)S(1)}, f32[512,512]{1,0:T(8,128)}) fusion(f32[16,512]{1,0:T(8,128)S(1)} %get-tuple-element.8, f32[16,512]{1,0:T(8,128)S(1)} %get-tuple-element.18, f32[16,512]{1,0:T(8,128)} %get-tuple-element.7, f32[512]{0:T(512)S(1)} %iota_add_fusion), kind=kLoop, calls=%fused_computation.5 | loop fusion | flops 24641536 | bytes 2197504 | tf_op jit(solution)/shard_map/reduce_sum | solution.py:43
  326.7 16.8 %gather_fusion = f32[4096,512]{1,0:T(8,128)} fusion(f32[512,512]{1,0:T(8,128)S(1)} %get-tuple-element.5, s32[4096]{0:T(1024)S(1)} %broadcast_clamp_fusion), kind=kCustom, calls=%fused_computation | custom fusion | bytes 16793600 | tf_op jit(solution)/shard_map/gather | solution.py:52
  343.5 16.3 %copy.17 = f32[64,64,512]{1,0,2:T(8,128)} copy(f32[64,64,512]{2,1,0:T(8,128)} %bitcast.55) | data formatting | bytes 16777216 | tf_op jit(solution)/shard_map/gather | solution.py:52
  359.8 0.0 copy-start.7
  359.8 0.0 copy-start.9
  359.8 8.3 %fusion.22 = f32[16,512,8]{0,2,1:T(8,128)} fusion(f32[8,64,512]{1,0,2:T(8,128)S(1)} %copy.18, f32[64]{0:T(128)S(1)} %iota_subtract_fusion.2, f32[16,512]{0,1:T(8,128)S(1)} %copy.20), kind=kOutput, calls=%fused_computation.36 | convolution fusion | flops 50855936 | bytes 1343744 | tf_op jit(solution)/shard_map/rsc,jsc->jrc/dot_general | solution.py:56
  368.1 2.2 copy.38
  370.2 0.0 copy-done.7
  370.2 0.0 copy-done.9
  370.2 0.5 multiply_reduce_fusion.3
  370.8 2.0 copy.30
  372.8 0.0 copy-start.3
  372.8 0.0 copy-start.4
  372.8 29.1 %fusion = f32[512,8,64]{2,1,0:T(8,128)S(1)} fusion(f32[8,64,512]{1,0,2:T(8,128)S(1)} %copy.18, f32[64,64,512]{1,0,2:T(8,128)} %copy.17, pred[64,64]{1,0:T(8,128)(4,1)S(1)} %subtract_compare_fusion), kind=kOutput, calls=%fused_computation.3 | convolution fusion | flops 203423744 | bytes 10489856 | tf_op jit(solution)/shard_map/tsc,jsc->jtc/dot_general | solution.py:53
  401.9 0.0 copy-done.3
  401.9 0.0 copy-done.4
  401.9 4.2 add_bitcast_fusion
  406.1 0.0 copy-start.8
  406.1 0.0 copy-start.1
  406.1 1.7 copy.22
  407.8 0.0 copy-done.8
  407.8 3.9 fusion.30
  411.7 0.0 copy-done.1
  (16 shorter events, 0.1 us)
Async XLA Ops:
  6.5 169.1 %copy-start = (bf16[512,1024]{1,0:T(8,128)(2,1)S(1)}, bf16[512,1024]{1,0:T(8,128)(2,1)}, u32[]{:S(2)}) copy-start(bf16[512,1024]{1,0:T(8,128)(2,1)} %param.6) | copy-start | bytes 3145732
  6.5 169.1 %all-gather.3.cloned.1.call-start = ((), (), s32[]{:S(2)}) async-start(), calls=%async_computation.1 | async-start | bytes 26738688 | tf_op jit(solution)/shard_map/all_gather | solution.py:21
  7.3 264.3 %reduce-scatter.2.cloned.1.call-start = ((), (), s32[]{:S(2)}) async-start(), calls=%async_computation.2 | async-start | bytes 14155776 | tf_op jit(solution)/shard_map/reduce_scatter | solution.py:24
  199.3 0.9 copy-start.6
  199.3 1.0 copy-start.5
  272.3 4.9 %collective-permute-start = (bf16[6,3,512]{2,0,1:T(8,128)(2,1)S(1)}, bf16[6,3,512]{2,0,1:T(8,128)(2,1)S(1)}, u32[]{:S(2)}, u32[]{:S(2)}) collective-permute-start(bf16[6,3,512]{2,0,1:T(8,128)(2,1)S(1)} %slice.74), channel_id=1, source_target_pairs={{0,8},{8,16},{16,24},{24,32},{32,40},{40,48},{48,56},{56,64},{64,7... | collective-permute-start | bytes 55304 | tf_op jit(solution)/shard_map/ppermute | solution.py:13
  281.7 1.7 copy-start.2
  359.8 10.5 %copy-start.7 = (f32[16,512]{1,0:T(8,128)S(1)}, f32[16,512]{1,0:T(8,128)}, u32[]{:S(2)}) copy-start(f32[16,512]{1,0:T(8,128)} %get-tuple-element.16) | copy-start | bytes 98308
  359.8 10.5 %copy-start.9 = (pred[8,8]{1,0:T(8,128)(4,1)S(1)}, pred[8,8]{1,0:T(8,128)(4,1)}, u32[]{:S(2)}) copy-start(pred[8,8]{1,0:T(8,128)(4,1)} %fusion.35) | copy-start | bytes 196
  372.8 29.1 %copy-start.3 = (f32[16,512,8]{0,2,1:T(8,128)S(1)}, f32[16,512,8]{0,2,1:T(8,128)}, u32[]{:S(2)}) copy-start(f32[16,512,8]{0,2,1:T(8,128)} %copy.30) | copy-start | bytes 786436
  372.8 29.1 %copy-start.4 = (f32[16,512]{0,1:T(8,128)S(1)}, f32[16,512]{0,1:T(8,128)}, u32[]{:S(2)}) copy-start(f32[16,512]{0,1:T(8,128)} %copy.19) | copy-start | bytes 98308
  406.1 1.7 copy-start.8
  406.1 5.6 %copy-start.1 = (bf16[512,1024]{1,0:T(8,128)(2,1)S(1)}, bf16[512,1024]{1,0:T(8,128)(2,1)}, u32[]{:S(2)}) copy-start(bf16[512,1024]{1,0:T(8,128)(2,1)} %param.6) | copy-start | bytes 3145732
Sparse Core Ops, SparseCore 0:
  9.5 166.0 all-gather.2
  199.4 72.0 reduce-scatter.1
where the time goes:
time: 419 us
  waiting for transfers between devices  242 us (58%)
  matrix products  65.3 us (16%)
  local copies, waits for them, and re-layouts  42.8 us (10%)
  blocking collectives  28.4 us (7%)
  other arithmetic  23.4 us (6%)
  between operations  13.6 us (3%)
    all_gather x1, waiting for transfers between devices, on_device(): lax.all_gather(in_weight, 'ctx', axis=2, tiled=True)  168 us
    reduce_scatter x1, waiting for transfers between devices, on_device(): lax.psum_scatter(partial_value.astype(jnp.bfloat16), 'ch', scatter_dimens...  71.2 us
    gather x2, local copies, waits for them, and re-layouts, on_device(): kernel[jnp.maximum(lag_steps, 0)]  33.1 us
    dot_general x1, matrix products, on_device(): within = jnp.einsum('tsc,jsc->jtc', toeplitz, pieces, precision=highest)  29.1 us
    all_gather x1, blocking collectives, on_device(): lax.all_gather(end_state[None].astype(jnp.bfloat16), 'ctx', axis=0, tiled...  28.4 us
    dot_general x1, matrix products, on_device(): jnp.einsum('td,dmg->tmg', tokens, lax.all_gather(in_weight, 'ctx', axis=2...  23.7 us
  transfers between devices with their start and end apart: 3, of which 3 were waited for; matrix products, arithmetic and copies ran while one was open for 0% of the time, Pallas kernels for 0%

commit v1 on v0

--- a/solution.py
+++ b/solution.py
@@ -67,9 +67,12 @@
     local_conv = within.reshape(length, channels)
     tail_decay = jnp.exp(-decay_rate[:, None, :] * (length - 1.0 - offsets)[None, :, None])
     end_state = jnp.sum(tail_decay * source[None, :, :], axis=1)
-    states = lax.all_gather(end_state[None].astype(jnp.bfloat16), "ctx", axis=0, tiled=True).astype(
-        jnp.float32
-    )
+    states = jnp.concatenate(
+        lax.all_to_all(
+            jnp.stack([end_state[None].astype(jnp.bfloat16)] * lax.axis_size("ctx")), "ctx", 0, 0
+        ),
+        axis=0,
+    ).astype(jnp.float32)
     position = lax.axis_index("ctx")
     earlier_ids = jnp.arange(states.shape[0], dtype=jnp.int32)
     distance = jnp.maximum(position - 1 - earlier_ids, 0).astype(jnp.float32)

time: 419 us -> 400 us (0.955)
  blocking collectives: 28.4 us -> 0 us
  starting transfers between devices: 3.42 us -> 11.1 us
    all_gather x1 -> x0, blocking collectives: 28.4 us -> none  [on_device(): lax.all_gather(end_state[None].astype(jnp.bfloat16), 'ctx', axis=0, tiled...]
    all_to_all x0 -> x1, starting transfers between devices: none -> 7.7 us  [on_device(): lax.all_to_all(jnp.stack([end_state[None].astype(jnp.bfloat16)] * lax.axi...]
  transfers between devices with their start and end apart: 3 -> 4, of which waited for: 3 -> 3; matrix products, arithmetic and copies ran while one was open for 0% -> 3% of each run, Pallas kernels for 0% -> 0%
where the time goes in v1:
time: 400 us; the launch traced here: 399 us
  waiting for transfers between devices  242 us (60%)
  matrix products  65.3 us (16%)
  local copies, waits for them, and re-layouts  44.3 us (11%)
  other arithmetic  22.6 us (6%)
  between operations  13.7 us (3%)
  starting transfers between devices  11.1 us (3%)
    all_gather x1, waiting for transfers between devices, on_device(): lax.all_gather(in_weight, 'ctx', axis=2, tiled=True)  168 us
    reduce_scatter x1, waiting for transfers between devices, on_device(): lax.psum_scatter(partial_value.astype(jnp.bfloat16), 'ch', scatter_dimens...  71.2 us
    gather x2, local copies, waits for them, and re-layouts, on_device(): kernel[jnp.maximum(lag_steps, 0)]  33.1 us
    dot_general x1, matrix products, on_device(): within = jnp.einsum('tsc,jsc->jtc', toeplitz, pieces, precision=highest)  29.1 us
    dot_general x1, matrix products, on_device(): jnp.einsum('td,dmg->tmg', tokens, lax.all_gather(in_weight, 'ctx', axis=2...  23.7 us
    dot_general x1, matrix products, on_device(): block_ends = jnp.einsum('rsc,jsc->jrc', closing, pieces, precision=highest)  8.29 us
  transfers between devices with their start and end apart: 4, of which 3 were waited for; matrix products, arithmetic and copies ran while one was open for 3% of the time, Pallas kernels for 0%

profile of v1, /device:TPU:0, one launch (start us, length us, event | category | flops | bytes accessed | tf_op | source)
XLA Modules:
  0.0 398.5 jit_solution(9055673827298107219)
XLA Ops:
  6.5 0.0 copy-start
  6.5 0.0 all-gather.2.cloned.1.call-start
  6.5 0.7 all-gather.2.cloned.1.call-update
  7.3 0.0 reduce-scatter.2.cloned.1.call-start
  7.3 168.3 %all-gather.2.cloned.1.call-done = bf16[1024,3,4096]{2,0,1:T(8,128)(2,1)} async-done(((bf16[1024,3,256]{2,0,1:T(8,128)(2,1)}), bf16[1024,3,4096]{2,0,1:T(8,128)(2,1)}) %all-gather.2.cloned.1.call-update) | async-done | bytes 25165840 | tf_op jit(solution)/shard_map/all_gather | solution.py:21
  175.6 0.0 copy-done
  175.6 23.7 %convolution_convert_fusion = bf16[512,3,4096]{2,0,1:T(8,128)(2,1)} fusion(bf16[1024,3,4096]{2,0,1:T(8,128)(2,1)} %all-gather.2.cloned.1.call-done, bf16[512,1024]{1,0:T(8,128)(2,1)S(1)} %copy-done), kind=kOutput, calls=%fused_computation.6 | convolution fusion | flops 12891193344 | bytes 38797312 | tf_op jit(solution)/shard_map/td,dmg->tmg/dot_general | solution.py:18
  199.3 0.0 copy-start.7
  199.3 0.0 copy-start.6
  199.3 0.0 reduce-scatter.2.cloned.1.call-update
  199.4 0.1 reshape.143
  199.5 0.7 fusion.35
  200.2 0.1 maximum_convert_fusion.1
  200.3 0.0 copy-done.7
  200.3 0.0 copy-done.6
  200.4 71.2 %reduce-scatter.2.cloned.1.call-done = bf16[512,3,512]{2,0,1:T(8,128)(2,1)} async-done(((bf16[512,3,4096]{2,0,1:T(8,128)(2,1)}), bf16[512,3,512]{2,0,1:T(8,128)(2,1)}) %reduce-scatter.2.cloned.1.call-update) | async-done | bytes 1572880 | tf_op jit(solution)/shard_map/reduce_scatter | solution.py:24
  271.6 0.7 slice.74
  272.3 3.4 collective-permute-start
  275.7 0.1 copy.26
  275.8 1.3 collective-permute-done
  277.2 1.9 maximum_convert_fusion
  279.1 2.6 fusion.10
  281.7 0.0 copy-start.2
  281.7 0.2 fusion.42
  281.9 0.2 slice_multiply_fusion.7
  282.1 1.3 copy-done.2
  283.4 2.9 multiply_reduce_fusion.1
  286.3 0.7 stack.2
  287.0 7.7 %all-to-all-start = ((bf16[16,1,16,512]{3,2,1,0:T(8,128)(2,1)}), bf16[16,1,16,512]{3,2,1,0:T(8,128)(2,1)}, u32[]{:S(2)}, u32[]{:S(2)}) async-start(bf16[16,1,16,512]{3,2,1,0:T(8,128)(2,1)} %stack.2), calls=%async_computation.1 | async-start | bytes 524288 | tf_op jit(solution)/shard_map/all_to_all | solution.py:71
  294.7 0.8 copy.24
  295.5 0.0 copy-start.8
  295.5 8.3 %fusion.22 = f32[16,512,8]{0,2,1:T(8,128)} fusion(f32[8,64,512]{1,0,2:T(8,128)S(1)} %copy.24, f32[64]{0:T(128)S(1)} %iota_subtract_fusion.2, f32[16,512]{0,1:T(8,128)S(1)} %copy.26), kind=kOutput, calls=%fused_computation.36 | convolution fusion | flops 50855936 | bytes 1343744 | tf_op jit(solution)/shard_map/rsc,jsc->jrc/dot_general | solution.py:56
  303.8 2.9 copy.44
  306.7 0.0 all-to-all-done
  306.7 1.1 fusion.34
  307.8 0.0 copy-done.8
  307.8 0.6 fusion.37
  308.5 0.8 copy.25
  309.3 7.8 %multiply_reduce_fusion.2 = (f32[512,512]{1,0:T(8,128)S(1)}, f32[512,512]{1,0:T(8,128)}) fusion(f32[16,512]{1,0:T(8,128)S(1)} %get-tuple-element.8, f32[16,512]{1,0:T(8,128)S(1)} %get-tuple-element.18, f32[16,512]{1,0:T(8,128)} %get-tuple-element.7, f32[512]{0:T(512)S(1)} %iota_add_fusion), kind=kLoop, calls=%fused_computation.5 | loop fusion | flops 24641536 | bytes 2197504 | tf_op jit(solution)/shard_map/reduce_sum | solution.py:43
  317.1 16.8 %gather_fusion = f32[4096,512]{1,0:T(8,128)} fusion(f32[512,512]{1,0:T(8,128)S(1)} %get-tuple-element.5, s32[4096]{0:T(1024)S(1)} %broadcast_clamp_fusion), kind=kCustom, calls=%fused_computation | custom fusion | bytes 16793600 | tf_op jit(solution)/shard_map/gather | solution.py:52
  333.9 0.0 copy-start.5
  333.9 0.0 copy-start.9
  333.9 0.0 copy-start.11
  333.9 16.3 %copy.23 = f32[64,64,512]{1,0,2:T(8,128)} copy(f32[64,64,512]{2,1,0:T(8,128)} %bitcast.56) | data formatting | bytes 16777216 | tf_op jit(solution)/shard_map/gather | solution.py:52
  350.2 0.0 copy-done.5
  350.2 0.0 copy-done.9
  350.2 0.0 copy-done.11
  350.2 0.5 multiply_reduce_fusion.3
  350.8 2.0 copy.36
  352.8 0.0 copy-start.3
  352.8 0.0 copy-start.4
  352.8 29.1 %fusion = f32[512,8,64]{2,1,0:T(8,128)S(1)} fusion(f32[8,64,512]{1,0,2:T(8,128)S(1)} %copy.24, f32[64,64,512]{1,0,2:T(8,128)} %copy.23, pred[64,64]{1,0:T(8,128)(4,1)S(1)} %subtract_compare_fusion), kind=kOutput, calls=%fused_computation.3 | convolution fusion | flops 203423744 | bytes 10489856 | tf_op jit(solution)/shard_map/tsc,jsc->jtc/dot_general | solution.py:53
  381.9 0.0 copy-done.3
  381.9 0.0 copy-done.4
  381.9 4.2 %add_bitcast_fusion = f32[8,64,512]{1,0,2:T(8,128)S(1)} fusion(f32[512,8,64]{2,1,0:T(8,128)S(1)} %fusion, f32[64]{0:T(128)S(1)} %iota_add_fusion.1, f32[16,512]{0,1:T(8,128)S(1)} %copy.26, f32[16,512,8]{0,2,1:T(8,128)S(1)} %copy-done.3, f32[16,512]{0,1:T(8,128)S(1)} %copy-done.4), kind=kOutput, calls=%fused_computation.30 | convolution fusion | flops 51183616 | bytes 2425088 | tf_op jit(solution)/shard_map/rtc,jrc->jtc/dot_general | solution.py:64
  386.1 0.0 copy-start.10
  386.1 0.0 copy-start.1
  386.1 1.7 copy.28
  387.8 0.0 copy-done.10
  387.8 3.9 fusion.30
  391.7 0.0 copy-done.1
  (16 shorter events, 0.1 us)
Async XLA Ops:
  6.5 169.1 %copy-start = (bf16[512,1024]{1,0:T(8,128)(2,1)S(1)}, bf16[512,1024]{1,0:T(8,128)(2,1)}, u32[]{:S(2)}) copy-start(bf16[512,1024]{1,0:T(8,128)(2,1)} %param.6) | copy-start | bytes 3145732
  6.5 169.1 %all-gather.2.cloned.1.call-start = ((), (), s32[]{:S(2)}) async-start(), calls=%async_computation.2 | async-start | bytes 26738688 | tf_op jit(solution)/shard_map/all_gather | solution.py:21
  7.3 264.3 %reduce-scatter.2.cloned.1.call-start = ((), (), s32[]{:S(2)}) async-start(), calls=%async_computation.3 | async-start | bytes 14155776 | tf_op jit(solution)/shard_map/reduce_scatter | solution.py:24
  199.3 0.9 copy-start.7
  199.3 1.0 copy-start.6
  272.3 4.9 %collective-permute-start = (bf16[6,3,512]{2,0,1:T(8,128)(2,1)S(1)}, bf16[6,3,512]{2,0,1:T(8,128)(2,1)S(1)}, u32[]{:S(2)}, u32[]{:S(2)}) collective-permute-start(bf16[6,3,512]{2,0,1:T(8,128)(2,1)S(1)} %slice.74), channel_id=1, source_target_pairs={{0,8},{8,16},{16,24},{24,32},{32,40},{40,48},{48,56},{56,64},{64,7... | collective-permute-start | bytes 55304 | tf_op jit(solution)/shard_map/ppermute | solution.py:13
  281.7 1.7 copy-start.2
  287.0 19.6 %all-to-all-start = ((bf16[16,1,16,512]{3,2,1,0:T(8,128)(2,1)}), bf16[16,1,16,512]{3,2,1,0:T(8,128)(2,1)}, u32[]{:S(2)}, u32[]{:S(2)}) async-start(bf16[16,1,16,512]{3,2,1,0:T(8,128)(2,1)} %stack.2), calls=%async_computation.1 | async-start | bytes 524288 | tf_op jit(solution)/shard_map/all_to_all | solution.py:71
  295.5 12.3 %copy-start.8 = (f32[16,512]{1,0:T(8,128)S(1)}, f32[16,512]{1,0:T(8,128)}, u32[]{:S(2)}) copy-start(f32[16,512]{1,0:T(8,128)} %param.9) | copy-start | bytes 98308
  333.9 16.3 %copy-start.5 = (f32[16,512,8]{1,0,2:T(8,128)S(1)}, f32[16,512,8]{1,0,2:T(8,128)}, u32[]{:S(2)}) copy-start(f32[16,512,8]{1,0,2:T(8,128)} %copy.44) | copy-start | bytes 786436
  333.9 16.3 %copy-start.9 = (f32[16,512]{1,0:T(8,128)S(1)}, f32[16,512]{1,0:T(8,128)}, u32[]{:S(2)}) copy-start(f32[16,512]{1,0:T(8,128)} %get-tuple-element.16) | copy-start | bytes 98308
  333.9 16.3 %copy-start.11 = (pred[8,8]{1,0:T(8,128)(4,1)S(1)}, pred[8,8]{1,0:T(8,128)(4,1)}, u32[]{:S(2)}) copy-start(pred[8,8]{1,0:T(8,128)(4,1)} %fusion.35) | copy-start | bytes 196
  352.8 29.1 %copy-start.3 = (f32[16,512,8]{0,2,1:T(8,128)S(1)}, f32[16,512,8]{0,2,1:T(8,128)}, u32[]{:S(2)}) copy-start(f32[16,512,8]{0,2,1:T(8,128)} %copy.36) | copy-start | bytes 786436
  352.8 29.1 %copy-start.4 = (f32[16,512]{0,1:T(8,128)S(1)}, f32[16,512]{0,1:T(8,128)}, u32[]{:S(2)}) copy-start(f32[16,512]{0,1:T(8,128)} %copy.25) | copy-start | bytes 98308
  386.1 1.7 copy-start.10
  386.1 5.6 %copy-start.1 = (bf16[512,1024]{1,0:T(8,128)(2,1)S(1)}, bf16[512,1024]{1,0:T(8,128)(2,1)}, u32[]{:S(2)}) copy-start(bf16[512,1024]{1,0:T(8,128)(2,1)} %param.6) | copy-start | bytes 3145732
Sparse Core Ops, SparseCore 0:
  9.5 166.0 all-gather.1
  199.5 72.0 reduce-scatter.1
